TPU v7x, 32 devices: a whole 2x2x4 slice. The times are simulated.
32 devices in a mesh: groups: 2 (over x), heads: 16 (over z, y, core).
Axes of the slice: x: 2, y: 2, z: 4, core: 2. Of those that a mesh axis runs over, the one named last changes fastest.
Arguments:
- q_codes: bfloat16 [1536, 6, 2048], P('heads', 'groups'), parts along dimension 1, may hold values from -6 to 6
- k_codes: bfloat16 [512, 6, 2048], P('heads', 'groups'), parts along dimension 1, may hold values from -6 to 6
- q_exps: int32 [6, 12, 16], P('groups'), parts along dimension 0, may hold values from -4 to -1
- k_exps: int32 [6, 4, 16], P('groups'), parts along dimension 0, may hold values from -4 to -1
- shard_of_host: int32 [16], replicated, may hold values from 0 to 15, each once
- head_owner: int32 [16], replicated, may hold values from 0 to 15, each once
Outputs:
- absorbed: bfloat16 [32, 6, 1536, 512], P('heads', 'groups'), parts along dimension 1
There are 2 independent parts, one for each index of `groups`. A program takes and returns all parts, laid end to end along the dimension named above; an argument that names none is the same for every part. Nothing has to cross between parts.
Inputs may be any that keep to these rules, and one draw needn't show every extreme that they name: `shard_of_host`: each shard is held by exactly one host. `head_owner`: each device owns exactly one head.
All inputs are finite; a program needn't handle non-finite values.
Results may differ from a plain program's by a relative error of at most 0.001.
Values may be sent and summed in bfloat16 or wider, within the bound.
A program may use at most 64 MiB of HBM per device.

v0:
```python
import jax
import jax.numpy as jnp
from jax import lax
from jax.sharding import PartitionSpec as P

BLK = 128


def swapped(block, axis, apart):
    count = lax.axis_size(axis)
    route = []
    for low in range(count):
        high = low | 1 << apart
        if high != low and high < count:
            route += [(low, high), (high, low)]
    return lax.ppermute(block, axis, route)


def dequant(codes, exps, shard):
    rows, layers, width = codes.shape
    heads = exps.shape[2]
    blocks = (shard * rows + jnp.arange(rows, dtype=jnp.int32)) // BLK
    expo = jnp.take(exps, blocks, axis=1).transpose(1, 0, 2).astype(jnp.float32)
    values = codes.astype(jnp.float32).reshape(rows, layers, heads, width // heads)
    return (values * jnp.exp2(expo)[..., None]).astype(jnp.bfloat16)


def per_device(q_codes, k_codes, q_exps, k_exps, shard_of_host, head_owner):
    count = lax.axis_size("heads")
    half = count // 2
    mine = lax.axis_index("heads")
    order = jnp.arange(count, dtype=jnp.int32)
    holder = jnp.zeros((count,), jnp.int32).at[shard_of_host].set(order)
    owned = jnp.zeros((count,), jnp.int32).at[head_owner].set(order)
    shard = shard_of_host[mine]
    q_weight = dequant(q_codes, q_exps, shard)
    k_weight = dequant(k_codes, k_exps, shard)
    q_rows = q_codes.shape[0]
    k_rows = k_codes.shape[0]
    q_send = jnp.take(q_weight, owned, axis=2)
    k_send = jnp.take(k_weight, owned, axis=2)
    q_recv = lax.all_to_all(q_send, "heads", split_axis=2, concat_axis=0, tiled=True)
    k_recv = lax.all_to_all(k_send, "heads", split_axis=2, concat_axis=0, tiled=True)
    items = q_recv.shape[1]
    slots = q_recv.shape[2]
    head_size = q_recv.shape[3]
    q_file = jnp.take(q_recv.reshape(count, q_rows, items, slots, head_size), holder, axis=0)
    k_file = jnp.take(k_recv.reshape(count, k_rows, items, slots, head_size), holder, axis=0)
    q_file = q_file.reshape(count * q_rows, items, slots, head_size)
    k_file = k_file.reshape(count * k_rows, items, slots, head_size)
    result = jnp.einsum("qlhd,klhd->lhqk", q_file, k_file, preferred_element_type=jnp.float32)
    result = result.astype(jnp.bfloat16)
    own = result[:, 0]
    partner = swapped(own, "heads", count.bit_length() - 2)
    upper = mine >= half
    first = jnp.where(upper, partner, own)
    second = jnp.where(upper, own, partner)
    return jnp.stack([first, second], axis=0)


def solution(mesh):
    placed = (
        P("heads", "groups", None),
        P("heads", "groups", None),
        P("groups", None, None),
        P("groups", None, None),
        P(),
        P(),
    )
    return jax.shard_map(
        per_device,
        mesh=mesh,
        in_specs=placed,
        out_specs=P("heads", "groups", None, None),
        check_vma=False,
    )
```

profile of v0, /device:TPU:1, one launch (start us, length us, event | category | flops | bytes accessed | tf_op | source)
XLA Modules:
  0.0 284.4 jit_solution(11450674585502293102)
XLA Ops:
  0.0 0.0 copy-start
  0.0 1.2 dynamic_slice.3
  1.9 0.7 compare_select_fusion.5
  2.6 0.6 scatter_custom_fusion.1
  3.3 1.3 gather_fusion.3
  4.6 0.1 copy.20
  4.7 1.3 fusion.1
  6.0 0.6 gather_fusion.4
  6.6 0.8 select_bitcast_fusion.3
  7.5 0.0 copy-start.1
  7.5 7.5 %all-to-all-start.1 = ((bf16[32,3,16,128]{3,0,1,2:T(8,128)(2,1)}), bf16[32,3,16,128]{3,0,1,2:T(8,128)(2,1)S(1)}, u32[]{:S(2)}, u32[]{:S(2)}) async-start(bf16[32,3,16,128]{3,0,1,2:T(8,128)(2,1)} %select_bitcast_fusion.3), calls=%async_computation.1 | async-start | bytes 786432 | tf_op jit(solution)/shard_map/all_to_all | solution.py:43
  15.7 0.0 copy-done
  15.7 0.8 gather_fusion
  16.5 0.1 copy.17
  16.6 0.0 copy-done.1
  16.6 0.8 fusion
  17.4 0.8 gather_fusion.1
  18.2 1.2 select_bitcast_fusion.2
  19.4 0.0 copy-start.2
  19.4 7.5 %all-to-all-done.1 = bf16[32,3,16,128]{3,0,1,2:T(8,128)(2,1)S(1)} async-done(((bf16[32,3,16,128]{3,0,1,2:T(8,128)(2,1)}), bf16[32,3,16,128]{3,0,1,2:T(8,128)(2,1)S(1)}, u32[]{:S(2)}, u32[]{:S(2)}) %all-to-all-start.1) | async-done | bytes 393248 | tf_op jit(solution)/shard_map/all_to_all | solution.py:43
  26.9 3.9 %all-to-all-start = ((bf16[96,3,16,128]{3,0,1,2:T(8,128)(2,1)}), bf16[96,3,16,128]{3,0,1,2:T(8,128)(2,1)S(1)}, u32[]{:S(2)}, u32[]{:S(2)}) async-start(bf16[96,3,16,128]{3,0,1,2:T(8,128)(2,1)} %select_bitcast_fusion.2), calls=%async_computation | async-start | bytes 2359296 | tf_op jit(solution)/shard_map/all_to_all | solution.py:42
  30.8 0.0 copy-done.2
  30.8 0.6 scatter_custom_fusion
  31.4 0.1 broadcast_in_dim.92
  31.5 0.1 broadcast_in_dim.93
  31.6 0.1 broadcast_in_dim.81
  31.7 0.1 broadcast_in_dim.82
  31.8 0.6 gather_fusion.5
  32.4 0.1 bitcast_select_fusion.1
  32.6 23.7 %all-to-all-done = bf16[96,3,16,128]{3,0,1,2:T(8,128)(2,1)S(1)} async-done(((bf16[96,3,16,128]{3,0,1,2:T(8,128)(2,1)}), bf16[96,3,16,128]{3,0,1,2:T(8,128)(2,1)S(1)}, u32[]{:S(2)}, u32[]{:S(2)}) %all-to-all-start) | async-done | bytes 1179680 | tf_op jit(solution)/shard_map/all_to_all | solution.py:42
  56.3 0.8 gather_fusion.2
  57.1 0.1 copy.19
  57.2 0.3 bitcast_select_fusion
  57.5 3.6 %convolution_convert_fusion = bf16[3,1536,512]{2,1,0:T(8,128)(2,1)} fusion(bf16[1536,3,128]{2,0,1:T(8,128)(2,1)S(1)} %bitcast_select_fusion, bf16[512,3,128]{2,0,1:T(8,128)(2,1)S(1)} %bitcast_select_fusion.1), kind=kOutput, calls=%fused_computation.11 | convolution fusion | flops 606339072 | bytes 6291456 | tf_op jit(solution)/shard_map/qlhd,klhd->lhqk/dot_general | solution.py:51
  61.0 4.3 %collective-permute-start = (bf16[3,1536,512]{2,1,0:T(8,128)(2,1)}, bf16[3,1536,512]{2,1,0:T(8,128)(2,1)}, u32[]{:S(2)}, u32[]{:S(2)}) collective-permute-start(bf16[3,1536,512]{2,1,0:T(8,128)(2,1)} %convolution_convert_fusion), channel_id=1, source_target_pairs={{0,8},{8,0},{1,9},{9,1},{2,10},{10,2},{3,11},{11,3},{4,12},{12,4},... | collective-permute-start | bytes 14155784 | tf_op jit(solution)/shard_map/ppermute | solution.py:16
  65.3 202.7 %collective-permute-done = bf16[3,1536,512]{2,1,0:T(8,128)(2,1)} collective-permute-done((bf16[3,1536,512]{2,1,0:T(8,128)(2,1)}, bf16[3,1536,512]{2,1,0:T(8,128)(2,1)}, u32[]{:S(2)}, u32[]{:S(2)}) %collective-permute-start) | collective-permute-done | bytes 4718624 | tf_op jit(solution)/shard_map/ppermute | solution.py:16
  268.0 8.0 %select_bitcast_fusion.1 = (bf16[1,3,1536,512]{3,2,1,0:T(8,128)(2,1)}, bf16[1,3,1536,512]{3,2,1,0:T(8,128)(2,1)}) fusion(bf16[3,1536,512]{2,1,0:T(8,128)(2,1)} %collective-permute-done, bf16[3,1536,512]{2,1,0:T(8,128)(2,1)} %convolution_convert_fusion, pred[]{:T(512)S(6)} %ge.35), kind=kLoop, calls=%fused_computation.10 | loop fusion | flops 4718592 | bytes 18874368 | tf_op jit(solution)/shard_map/stack | solution.py:58
  276.1 8.4 %pad_maximum_fusion = bf16[2,3,1536,512]{3,2,1,0:T(8,128)(2,1)} fusion(bf16[1,3,1536,512]{3,2,1,0:T(8,128)(2,1)} %get-tuple-element.6, bf16[1,3,1536,512]{3,2,1,0:T(8,128)(2,1)} %get-tuple-element.5), kind=kLoop, calls=%fused_computation.8 | loop fusion | flops 4718592 | bytes 18874368 | tf_op jit(solution)/shard_map/stack | solution.py:58
  (18 shorter events, 0.2 us)
Async XLA Ops:
  0.0 15.7 %copy-start = (s32[3,12,16]{2,1,0:T(8,128)S(1)}, s32[3,12,16]{2,1,0:T(8,128)}, u32[]{:S(2)}) copy-start(s32[3,12,16]{2,1,0:T(8,128)} %param.8) | copy-start | bytes 6916
  7.5 9.1 %copy-start.1 = (bf16[96,3,2048]{2,0,1:T(8,128)(2,1)S(1)}, bf16[96,3,2048]{2,0,1:T(8,128)(2,1)}, u32[]{:S(2)}) copy-start(bf16[96,3,2048]{2,0,1:T(8,128)(2,1)} %param.6) | copy-start | bytes 3538948
  7.5 19.4 %all-to-all-start.1 = ((bf16[32,3,16,128]{3,0,1,2:T(8,128)(2,1)}), bf16[32,3,16,128]{3,0,1,2:T(8,128)(2,1)S(1)}, u32[]{:S(2)}, u32[]{:S(2)}) async-start(bf16[32,3,16,128]{3,0,1,2:T(8,128)(2,1)} %select_bitcast_fusion.3), calls=%async_computation.1 | async-start | bytes 786432 | tf_op jit(solution)/shard_map/all_to_all | solution.py:43
  19.4 11.4 %copy-start.2 = (s32[16]{0:T(128)S(1)}, s32[16]{0:T(128)}, u32[]{:S(2)}) copy-start(s32[16]{0:T(128)} %param.10) | copy-start | bytes 196
  26.9 29.4 %all-to-all-start = ((bf16[96,3,16,128]{3,0,1,2:T(8,128)(2,1)}), bf16[96,3,16,128]{3,0,1,2:T(8,128)(2,1)S(1)}, u32[]{:S(2)}, u32[]{:S(2)}) async-start(bf16[96,3,16,128]{3,0,1,2:T(8,128)(2,1)} %select_bitcast_fusion.2), calls=%async_computation | async-start | bytes 2359296 | tf_op jit(solution)/shard_map/all_to_all | solution.py:42
  61.0 207.0 %collective-permute-start = (bf16[3,1536,512]{2,1,0:T(8,128)(2,1)}, bf16[3,1536,512]{2,1,0:T(8,128)(2,1)}, u32[]{:S(2)}, u32[]{:S(2)}) collective-permute-start(bf16[3,1536,512]{2,1,0:T(8,128)(2,1)} %convolution_convert_fusion), channel_id=1, source_target_pairs={{0,8},{8,0},{1,9},{9,1},{2,10},{10,2},{3,11},{11,3},{4,12},{12,4},... | collective-permute-start | bytes 14155784 | tf_op jit(solution)/shard_map/ppermute | solution.py:16
where the time goes:
time: 286 us; the launch traced here: 284 us
  waiting for transfers between devices  234 us (82%)
  other arithmetic  21.8 us (8%)
  starting transfers between devices  15.6 us (5%)
  local copies, waits for them, and re-layouts  8.03 us (3%)
  matrix products  3.58 us (1%)
    ppermute x1, waiting for transfers between devices, swapped(): return lax.ppermute(block, axis, route)  203 us
    all_to_all x1, waiting for transfers between devices, per_device(): lax.all_to_all(q_send, 'heads', split_axis=2, concat_axis=0, tiled=True)  23.7 us
    another operation x2, other arithmetic, per_device(): return jnp.stack([first, second], axis=0)  16.4 us
    all_to_all x1, starting transfers between devices, per_device(): lax.all_to_all(k_send, 'heads', split_axis=2, concat_axis=0, tiled=True)  7.48 us
    all_to_all x1, waiting for transfers between devices, per_device(): lax.all_to_all(k_send, 'heads', split_axis=2, concat_axis=0, tiled=True)  7.48 us
  transfers between devices with their start and end apart: 3, of which 3 were waited for; matrix products, arithmetic and copies ran while one was open for 2% of the time, Pallas kernels for 0%

commit v1 on v0

v1 whole, which is shorter than its diff:
```python
import functools
import math

import jax
import jax.numpy as jnp
from jax import lax
from jax.experimental import pallas as pl
from jax.experimental.pallas import tpu as pltpu
from jax.sharding import PartitionSpec as P

BLK = 128
MESH = pl.DeviceIdType.MESH


def exchange(n, q_ref, k_ref, table_ref, owned_ref, out_ref, scaled, send_buf, send_sem, recv_sem, own_sem):
    half = n // 2
    me = lax.axis_index("heads")
    layers, q_rows, _ = q_ref.shape
    k_rows = k_ref.shape[1]
    lower = lax.rem(me, half)
    mine = me - lower
    other = half - mine

    barrier = pltpu.get_barrier_semaphore()

    def greet(i, carry):
        pl.semaphore_signal(barrier, inc=1, device_id={"heads": lax.rem(me + i, n)}, device_id_type=MESH)
        return carry

    lax.fori_loop(1, n, greet, 0)
    q_chunks = q_rows // math.gcd(q_rows, BLK)

    def part(ref, layer, head, rows, first):
        unit = math.gcd(rows, BLK)
        values = ref[layer, :, pl.ds(pl.multiple_of(head * 128, 128), 128)].astype(jnp.float32)
        pieces = []
        for c in range(rows // unit):
            expo = table_ref[layer, first + c, head]
            scale = jnp.exp2(jnp.full((8, 128), expo, jnp.int32).astype(jnp.float32))
            piece = values[c * unit : (c + 1) * unit].reshape(unit // 8, 8, 128) * scale[None]
            pieces.append(piece.reshape(unit, 128))
        return pieces

    def weigh(head, carry):
        for layer in range(layers):
            pieces = part(q_ref, layer, head, q_rows, 0) + part(k_ref, layer, head, k_rows, q_chunks)
            scaled[head, layer] = jnp.concatenate(pieces, axis=0).astype(jnp.bfloat16)
        return carry

    lax.fori_loop(0, n, weigh, 0)

    def prepare(t):
        for slot in range(2):
            send_buf[t, slot] = scaled[owned_ref[t + slot * half]]

    def remote(t, to):
        return pltpu.make_async_remote_copy(
            src_ref=send_buf.at[t],
            dst_ref=out_ref.at[me],
            send_sem=send_sem.at[to],
            recv_sem=recv_sem.at[me],
            device_id={"heads": to},
            device_id_type=MESH,
        )

    prepare(lower)
    pl.semaphore_wait(barrier, n - 1)
    remote(lower, lower + other).start()
    own = pltpu.make_async_copy(send_buf.at[lower], out_ref.at[me], own_sem)
    own.start()

    def far(i, carry):
        t = lax.rem(lower + i, half)
        prepare(t)
        remote(t, t + other).start()
        return carry

    lax.fori_loop(1, half, far, 0)

    def near(i, carry):
        t = lax.rem(lower + i, half)
        remote(t, t + mine).start()
        return carry

    lax.fori_loop(1, half, near, 0)

    def finish(i, carry):
        peer = lax.rem(me + i, n)
        copy = pltpu.make_async_remote_copy(
            src_ref=send_buf.at[lax.rem(peer, half)],
            dst_ref=out_ref.at[peer],
            send_sem=send_sem.at[peer],
            recv_sem=recv_sem.at[peer],
            device_id={"heads": peer},
            device_id_type=MESH,
        )
        copy.wait_send()
        copy.wait_recv()
        return carry

    lax.fori_loop(1, n, finish, 0)
    own.wait()


def absorb(n, q_rows, k_rows, splits, shard_ref, recv_ref, out_ref, q_file, k_file):
    @pl.when(pl.program_id(2) == 0)
    def _():
        for host in range(n):
            shard = shard_ref[host]
            block = recv_ref[host, 0, 0].astype(q_file.dtype)
            q_file[pl.ds(pl.multiple_of(shard * q_rows, q_rows), q_rows)] = block[:q_rows]
            k_file[pl.ds(pl.multiple_of(shard * k_rows, k_rows), k_rows)] = block[q_rows:]

    rows = n * q_rows // splits
    at = pl.multiple_of(pl.program_id(2) * rows, rows)
    out_ref[0, 0] = lax.dot_general(
        q_file[pl.ds(at, rows)].astype(jnp.bfloat16),
        k_file[...].astype(jnp.bfloat16),
        (((1,), (1,)), ((), ())),
        preferred_element_type=jnp.float32,
    ).astype(jnp.bfloat16)


def tables(q_rows, k_rows, q_exps, k_exps, shard, head_owner):
    heads = head_owner.shape[0]
    order = jnp.arange(heads, dtype=jnp.int32)
    q_unit, k_unit = math.gcd(q_rows, BLK), math.gcd(k_rows, BLK)
    q_blocks = q_exps.shape[1]
    every = jnp.concatenate([q_exps, k_exps], axis=1)
    blocks = [(shard * q_rows + at) // BLK for at in range(0, q_rows, q_unit)]
    blocks += [q_blocks + (shard * k_rows + at) // BLK for at in range(0, k_rows, k_unit)]
    at_block = jnp.stack(blocks)[:, None] == jnp.arange(every.shape[1], dtype=jnp.int32)[None]
    table = jnp.sum(jnp.where(at_block[None, :, :, None], every[:, None], 0), axis=2, dtype=jnp.int32)
    owned = jnp.sum(jnp.where(order[:, None] == head_owner[None], order[None], 0), axis=1, dtype=jnp.int32)
    return table, owned


def per_device(n, q_codes, k_codes, q_exps, k_exps, shard_of_host, head_owner):
    q_rows, layers, width = q_codes.shape
    k_rows = k_codes.shape[0]
    rows = q_rows + k_rows
    half = n // 2
    shard = shard_of_host[lax.axis_index("heads")]
    table, owned = tables(q_rows, k_rows, q_exps, k_exps, shard, head_owner)
    smem = pl.BlockSpec(memory_space=pltpu.SMEM)
    vmem = pl.BlockSpec(memory_space=pltpu.VMEM)
    received = pl.pallas_call(
        functools.partial(exchange, n),
        out_shape=jax.ShapeDtypeStruct((n, 2, layers, rows, 128), jnp.bfloat16),
        in_specs=[vmem, vmem, smem, smem],
        out_specs=pl.BlockSpec(memory_space=pl.ANY),
        scratch_shapes=[
            pltpu.VMEM((n, layers, rows, 128), jnp.bfloat16),
            pltpu.VMEM((half, 2, layers, rows, 128), jnp.bfloat16),
            pltpu.SemaphoreType.DMA((n,)),
            pltpu.SemaphoreType.DMA((n,)),
            pltpu.SemaphoreType.DMA,
        ],
        compiler_params=pltpu.CompilerParams(
            collective_id=0, has_side_effects=True, vmem_limit_bytes=24 * 2**20
        ),
    )(q_codes.transpose(1, 0, 2), k_codes.transpose(1, 0, 2), table, owned)

    splits = 2
    q_all, k_all = n * q_rows, n * k_rows
    held = jnp.bfloat16 if q_rows % 16 == 0 and k_rows % 16 == 0 else jnp.float32
    return pl.pallas_call(
        functools.partial(absorb, n, q_rows, k_rows, splits),
        out_shape=jax.ShapeDtypeStruct((2, layers, q_all, k_all), jnp.bfloat16),
        grid_spec=pltpu.PrefetchScalarGridSpec(
            num_scalar_prefetch=1,
            grid=(2, layers, splits),
            in_specs=[pl.BlockSpec((n, 1, 1, rows, 128), lambda a, b, c, shard: (0, a, b, 0, 0))],
            out_specs=pl.BlockSpec((1, 1, q_all // splits, k_all), lambda a, b, c, shard: (a, b, c, 0)),
            scratch_shapes=[pltpu.VMEM((q_all, 128), held), pltpu.VMEM((k_all, 128), held)],
        ),
        compiler_params=pltpu.CompilerParams(vmem_limit_bytes=24 * 2**20),
        cost_estimate=pl.CostEstimate(
            flops=2 * 2 * layers * q_all * k_all * 128,
            bytes_accessed=2 * layers * (q_all * k_all + n * rows * 128) * 2,
            transcendentals=0,
        ),
    )(shard_of_host, received)


def solution(mesh):
    placed = (
        P("heads", "groups", None),
        P("heads", "groups", None),
        P("groups", None, None),
        P("groups", None, None),
        P(),
        P(),
    )
    return jax.shard_map(
        functools.partial(per_device, mesh.shape["heads"]),
        mesh=mesh,
        in_specs=placed,
        out_specs=P("heads", "groups", None, None),
        check_vma=False,
    )
```

time: 286 us -> 94.3 us (0.33)
  waiting for transfers between devices: 234 us -> 0 us
  Pallas kernels: 0 us -> 87.2 us
  other arithmetic: 21.8 us -> 1.79 us
  starting transfers between devices: 15.6 us -> 0 us
  local copies, waits for them, and re-layouts: 8.03 us -> 3.57 us
  matrix products: 3.58 us -> 0 us
    ppermute x1 -> x0, waiting for transfers between devices: 203 us -> none  [swapped(): return lax.ppermute(block, axis, route)]
    pallas_call x0 -> x2, Pallas kernels: none -> 87.2 us  [the longest x1 78.4 us: per_device(): pl.pallas_call(functools.partial(exchange, n), out_shape=jax.ShapeDtypeSt...]
    all_to_all x2 -> x0, waiting for transfers between devices: 31.2 us -> none  [the longest x1 23.7 us: per_device(): lax.all_to_all(q_send, 'heads', split_axis=2, concat_axis=0, tiled=True)]
    another operation x2 -> x1, other arithmetic: 16.4 us -> 0.08 us  [tables(): jnp.stack(blocks)[:, None]]
    all_to_all x2 -> x0, starting transfers between devices: 11.4 us -> none  [the longest x1 7.48 us: per_device(): lax.all_to_all(k_send, 'heads', split_axis=2, concat_axis=0, tiled=True)]
    gather x10 -> x0, local copies, waits for them, and re-layouts: 5.2 us -> none  [the longest x4 2.29 us: dequant(): expo = jnp.take(exps, blocks, axis=1).transpose(1, 0, 2).astype(jnp.float32)]
    ppermute x1 -> x0, starting transfers between devices: 4.26 us -> none  [swapped(): return lax.ppermute(block, axis, route)]
    dot_general x1 -> x0, matrix products: 3.58 us -> none  [per_device(): jnp.einsum('qlhd,klhd->lhqk', q_file, k_file, preferred_element_type=jnp....]
  transfers between devices with their start and end apart: 3 -> 0, of which waited for: 3 -> 0; matrix products, arithmetic and copies ran while one was open for 2% -> 0% of each run, Pallas kernels for 0% -> 0%
where the time goes in v1:
time: 94.3 us; the launch traced here: 94 us
  Pallas kernels  87.2 us (92%)
  local copies, waits for them, and re-layouts  3.57 us (4%)
  other arithmetic  1.79 us (2%)
  between operations  1.41 us (1%)
    pallas_call x1, Pallas kernels, per_device(): pl.pallas_call(functools.partial(exchange, n), out_shape=jax.ShapeDtypeSt...  78.4 us
    pallas_call x1, Pallas kernels, per_device(): pl.pallas_call(functools.partial(absorb, n, q_rows, k_rows, splits), out_...  8.81 us
    unnamed x6, local copies, waits for them, and re-layouts  2.26 us

profile of v1, /device:TPU:1, one launch (start us, length us, event | category | flops | bytes accessed | tf_op | source)
XLA Modules:
  0.0 94.0 jit_solution(7361413921801556036)
XLA Ops:
  0.0 0.0 copy-start.2
  0.0 1.3 %dynamic_slice.3 = s32[1]{0:T(128)} dynamic-slice(s32[16]{0:T(128)} %shard_ref.1, s32[]{:T(128)S(6)} %select_n.25), dynamic_slice_sizes={1} | dynamic-slice | bytes 12 | tf_op jit(solution)/shard_map/dynamic_slice | solution.py:143
  2.7 0.1 pad_add_fusion.1
  2.8 0.1 iota_compare_fusion.1
  2.8 0.8 select_reduce_fusion.1.owned_ref
  3.6 0.8 pad_add_fusion
  4.4 0.1 select_reduce_fusion.table_ref
  4.5 0.0 copy-start
  4.5 1.3 %copy-done = bf16[96,3,2048]{2,0,1:T(8,128)(2,1)S(1)} copy-done((bf16[96,3,2048]{2,0,1:T(8,128)(2,1)S(1)}, bf16[96,3,2048]{2,0,1:T(8,128)(2,1)}, u32[]{:S(2)}) %copy-start) | copy-done | bytes 1179672
  5.8 0.0 copy-start.1
  5.8 1.0 %copy-done.1 = bf16[32,3,2048]{2,0,1:T(8,128)(2,1)S(1)} copy-done((bf16[32,3,2048]{2,0,1:T(8,128)(2,1)S(1)}, bf16[32,3,2048]{2,0,1:T(8,128)(2,1)}, u32[]{:S(2)}) %copy-start.1) | copy-done | bytes 393240
  6.8 78.4 %shard_map.64.recv_ref = bf16[16,2,3,128,128]{4,3,2,1,0:T(8,128)(2,1)S(1)} custom-call(bf16[3,96,2048]{2,1,0:T(8,128)(2,1)S(1)} %bitcast.8, bf16[3,32,2048]{2,1,0:T(8,128)(2,1)S(1)} %bitcast.9, s32[3,4,16]{2,1,0:T(4,128)S(1)} %select_reduce_fusion.table_ref, s32[16]{0:T(128)S(1)} %select_reduce_fusion.1.owned_ref), custom_call_target="tpu_custom_call" | custom-call | tf_op jit(solution)/shard_map/pallas_call | solution.py:147
  85.2 0.0 copy-done.2
  85.2 8.8 %shard_map.65 = bf16[2,3,1536,512]{3,2,1,0:T(8,128)(2,1)} custom-call(s32[16]{0:T(128)S(1)} %copy-done.2, bf16[16,2,3,128,128]{4,3,2,1,0:T(8,128)(2,1)S(1)} %shard_map.64.recv_ref), custom_call_target="tpu_custom_call" | custom-call | flops 1207959552 | bytes 12582912 | tf_op jit(solution)/shard_map/pallas_call | solution.py:167
Async XLA Ops:
  0.0 85.2 %copy-start.2 = (s32[16]{0:T(128)S(1)}, s32[16]{0:T(128)}, u32[]{:S(2)}) copy-start(s32[16]{0:T(128)} %shard_ref.1) | copy-start | bytes 196
  4.5 1.3 %copy-start = (bf16[96,3,2048]{2,0,1:T(8,128)(2,1)S(1)}, bf16[96,3,2048]{2,0,1:T(8,128)(2,1)}, u32[]{:S(2)}) copy-start(bf16[96,3,2048]{2,0,1:T(8,128)(2,1)} %param.6) | copy-start | bytes 3538948
  5.8 1.0 %copy-start.1 = (bf16[32,3,2048]{2,0,1:T(8,128)(2,1)S(1)}, bf16[32,3,2048]{2,0,1:T(8,128)(2,1)}, u32[]{:S(2)}) copy-start(bf16[32,3,2048]{2,0,1:T(8,128)(2,1)} %param.7) | copy-start | bytes 1179652

commit v2 on v0

v2 whole, which is shorter than its diff:
```python
import functools
import math

import jax
import jax.numpy as jnp
from jax import lax
from jax.experimental import pallas as pl
from jax.experimental.pallas import tpu as pltpu
from jax.sharding import PartitionSpec as P

BLK = 128
LANES = 128
ORDER = 1
MESH = pl.DeviceIdType.MESH
VMEM = pl.BlockSpec(memory_space=pltpu.VMEM)
SMEM = pl.BlockSpec(memory_space=pltpu.SMEM)
HBM = pl.BlockSpec(memory_space=pltpu.HBM)


def position(table_ref, n, value):
    found = jnp.int32(0)
    for at in range(n):
        found = jnp.where(table_ref[at] == value, jnp.int32(at), found)
    return found


def exchange(
    n, q_hbm, k_hbm, qe_ref, ke_ref, shard_ref, owner_ref, out_ref,
    q_in, k_in, q_scaled, k_scaled, q_send, k_send, q_recv, k_recv, k_file,
    in_sem, q_send_sem, k_send_sem, q_recv_sem, k_recv_sem,
):
    half = n // 2
    me = lax.axis_index("heads")
    layers, q_rows, _ = q_in.shape
    k_rows = k_in.shape[1]
    lower = lax.rem(me, half)
    mine = me - lower
    other = half - mine

    loads = [pltpu.make_async_copy(k_hbm, k_in, in_sem.at[0]), pltpu.make_async_copy(q_hbm, q_in, in_sem.at[1])]
    for load in loads:
        load.start()

    barrier = pltpu.get_barrier_semaphore()

    def greet(i, carry):
        pl.semaphore_signal(barrier, inc=1, device_id={"heads": lax.rem(me + i, n)}, device_id_type=MESH)
        return carry

    lax.fori_loop(1, n, greet, 0)

    shard = shard_ref[me]

    def weigh(source, exps_ref, target, rows, head):
        unit = math.gcd(rows, BLK)
        for layer in range(layers):
            values = source[layer, :, pl.ds(pl.multiple_of(head * LANES, LANES), LANES)].astype(jnp.float32)
            pieces = []
            for at in range(0, rows, unit):
                expo = exps_ref[layer, lax.div(shard * rows + at, BLK), head]
                scale = jnp.exp2(jnp.full((8, LANES), expo, jnp.int32).astype(jnp.float32))
                piece = values[at : at + unit].reshape(unit // 8, 8, LANES) * scale[None]
                pieces.append(piece.reshape(unit, LANES))
            target[head, layer] = jnp.concatenate(pieces, axis=0).astype(jnp.bfloat16)

    def weigh_k(head, carry):
        weigh(k_in, ke_ref, k_scaled, k_rows, head)
        return carry

    def weigh_q(head, carry):
        weigh(q_in, qe_ref, q_scaled, q_rows, head)
        return carry

    loads[0].wait()
    lax.fori_loop(0, n, weigh_k, 0)
    loads[1].wait()
    lax.fori_loop(0, n, weigh_q, 0)

    def prepare(t):
        for slot in range(2):
            head = position(owner_ref, n, t + slot * half)
            k_send[t, slot] = k_scaled[head]
            q_send[t, slot] = q_scaled[head]

    def copy(send, recv, send_sem, recv_sem, to, slot):
        return pltpu.make_async_remote_copy(
            src_ref=send.at[lax.rem(to, half)],
            dst_ref=recv.at[slot],
            send_sem=send_sem.at[to],
            recv_sem=recv_sem.at[slot],
            device_id={"heads": to},
            device_id_type=MESH,
        )

    q_copy = functools.partial(copy, q_send, q_recv, q_send_sem, q_recv_sem)
    k_copy = functools.partial(copy, k_send, k_recv, k_send_sem, k_recv_sem)

    prepare(lower)
    pl.semaphore_wait(barrier, n - 1)
    k_copy(lower + other, me).start()
    q_copy(lower + other, me).start()
    k_recv[me] = k_send[lower]
    q_recv[me] = q_send[lower]

    def far(i, carry):
        t = lax.rem(lower + i, half)
        prepare(t)
        k_copy(t + other, me).start()
        if ORDER == 0:
            q_copy(t + other, me).start()
        if ORDER == 1:
            k_copy(t + mine, me).start()
            q_copy(t + other, me).start()
            q_copy(t + mine, me).start()
        if ORDER == 2:
            k_copy(t + mine, me).start()
        return carry

    lax.fori_loop(1, half, far, 0)

    def near(i, carry):
        t = lax.rem(lower + i, half)
        if ORDER == 2:
            q_copy(t + other, me).start()
        if ORDER == 0:
            k_copy(t + mine, me).start()
        q_copy(t + mine, me).start()
        return carry

    if ORDER != 1:
        lax.fori_loop(1, half, near, 0)

    def k_arrival(i, carry):
        k_copy(0, lax.rem(me + i, n)).wait_recv()
        return carry

    lax.fori_loop(1, n, k_arrival, 0)
    holders = [position(shard_ref, n, s) for s in range(n)]
    for slot in range(2):
        for layer in range(layers):
            rows = [k_recv[holder, slot, layer].astype(jnp.float32) for holder in holders]
            k_file[slot, layer] = jnp.concatenate(rows, axis=0).astype(jnp.bfloat16)

    def multiply(host):
        for slot in range(2):
            for layer in range(layers):
                out_ref[host, slot, layer] = lax.dot_general(
                    q_recv[host, slot, layer],
                    k_file[slot, layer],
                    (((1,), (1,)), ((), ())),
                    preferred_element_type=jnp.float32,
                ).astype(jnp.bfloat16)

    def arrival(i, carry):
        here = mine + lax.rem(lower + half - i, half)
        there = other + lax.rem(lower + half - i, half)

        @pl.when(i > 0)
        def _():
            q_copy(0, here).wait_recv()

        multiply(here)
        q_copy(0, there).wait_recv()
        multiply(there)
        return carry

    lax.fori_loop(0, half, arrival, 0)

    def finish(i, carry):
        peer = lax.rem(me + i, n)
        k_copy(peer, 0).wait_send()
        q_copy(peer, 0).wait_send()
        return carry

    lax.fori_loop(1, n, finish, 0)


def place(n, shard_ref, products, out_ref, sem):
    rows = products.shape[3]

    def row_copy(host):
        at = pl.ds(pl.multiple_of(shard_ref[host] * rows, rows), rows)
        return pltpu.make_async_copy(products.at[host], out_ref.at[:, :, at, :], sem.at[host])

    for host in range(n):
        row_copy(host).start()
    for host in range(n):
        row_copy(host).wait()


def per_device(n, q_codes, k_codes, q_exps, k_exps, shard_of_host, head_owner):
    q_rows, layers, width = q_codes.shape
    k_rows = k_codes.shape[0]
    half = n // 2
    q_all, k_all = n * q_rows, n * k_rows
    sent = jnp.bfloat16
    products = pl.pallas_call(
        functools.partial(exchange, n),
        out_shape=pltpu.VMEM((n, 2, layers, q_rows, k_all), jnp.bfloat16),
        in_specs=[HBM, HBM, SMEM, SMEM, SMEM, SMEM],
        out_specs=VMEM,
        scratch_shapes=[
            pltpu.VMEM((layers, q_rows, width), sent),
            pltpu.VMEM((layers, k_rows, width), sent),
            pltpu.VMEM((n, layers, q_rows, LANES), sent),
            pltpu.VMEM((n, layers, k_rows, LANES), sent),
            pltpu.VMEM((half, 2, layers, q_rows, LANES), sent),
            pltpu.VMEM((half, 2, layers, k_rows, LANES), sent),
            pltpu.VMEM((n, 2, layers, q_rows, LANES), sent),
            pltpu.VMEM((n, 2, layers, k_rows, LANES), sent),
            pltpu.VMEM((2, layers, k_all, LANES), sent),
            pltpu.SemaphoreType.DMA((2,)),
            pltpu.SemaphoreType.DMA((n,)),
            pltpu.SemaphoreType.DMA((n,)),
            pltpu.SemaphoreType.DMA((n,)),
            pltpu.SemaphoreType.DMA((n,)),
        ],
        compiler_params=pltpu.CompilerParams(
            collective_id=0, has_side_effects=True, vmem_limit_bytes=40 * 2**20
        ),
    )(q_codes.transpose(1, 0, 2), k_codes.transpose(1, 0, 2), q_exps, k_exps, shard_of_host, head_owner)

    if q_rows % 16:
        order = jnp.arange(n, dtype=jnp.int32)
        holder = jnp.zeros((n,), jnp.int32).at[shard_of_host].set(order)
        filed = jnp.take(products, holder, axis=0)
        return filed.transpose(1, 2, 0, 3, 4).reshape(2, layers, q_all, k_all)
    return pl.pallas_call(
        functools.partial(place, n),
        out_shape=jax.ShapeDtypeStruct((2, layers, q_all, k_all), jnp.bfloat16),
        in_specs=[SMEM, VMEM],
        out_specs=HBM,
        scratch_shapes=[pltpu.SemaphoreType.DMA((n,))],
        compiler_params=pltpu.CompilerParams(vmem_limit_bytes=40 * 2**20),
    )(shard_of_host, products)


def solution(mesh):
    placed = (
        P("heads", "groups", None),
        P("heads", "groups", None),
        P("groups", None, None),
        P("groups", None, None),
        P(),
        P(),
    )
    return jax.shard_map(
        functools.partial(per_device, mesh.shape["heads"]),
        mesh=mesh,
        in_specs=placed,
        out_specs=P("heads", "groups", None, None),
        check_vma=False,
    )
```

time: 286 us -> 90.2 us (0.32)
  waiting for transfers between devices: 234 us -> 0 us
  Pallas kernels: 0 us -> 84.6 us
  other arithmetic: 21.8 us -> 0 us
  starting transfers between devices: 15.6 us -> 0 us
  matrix products: 3.58 us -> 0 us
  local copies, waits for them, and re-layouts: 8.03 us -> 5 us
    ppermute x1 -> x0, waiting for transfers between devices: 203 us -> none  [swapped(): return lax.ppermute(block, axis, route)]
    pallas_call x0 -> x2, Pallas kernels: none -> 84.6 us  [the longest x1 80.3 us: per_device(): pl.pallas_call(functools.partial(exchange, n), out_shape=pltpu.VMEM((n, 2...]
    all_to_all x2 -> x0, waiting for transfers between devices: 31.2 us -> none  [the longest x1 23.7 us: per_device(): lax.all_to_all(q_send, 'heads', split_axis=2, concat_axis=0, tiled=True)]
    another operation x2 -> x0, other arithmetic: 16.4 us -> none  [per_device(): return jnp.stack([first, second], axis=0)]
    all_to_all x2 -> x0, starting transfers between devices: 11.4 us -> none  [the longest x1 7.48 us: per_device(): lax.all_to_all(k_send, 'heads', split_axis=2, concat_axis=0, tiled=True)]
    gather x10 -> x0, local copies, waits for them, and re-layouts: 5.2 us -> none  [the longest x4 2.29 us: dequant(): expo = jnp.take(exps, blocks, axis=1).transpose(1, 0, 2).astype(jnp.float32)]
    unnamed x6 -> x12, local copies, waits for them, and re-layouts: 0.01 us -> 5 us
    ppermute x1 -> x0, starting transfers between devices: 4.26 us -> none  [swapped(): return lax.ppermute(block, axis, route)]
  transfers between devices with their start and end apart: 3 -> 0, of which waited for: 3 -> 0; matrix products, arithmetic and copies ran while one was open for 2% -> 0% of each run, Pallas kernels for 0% -> 0%
where the time goes in v2:
time: 90.2 us; the launch traced here: 89.6 us
  Pallas kernels  84.6 us (94%)
  local copies, waits for them, and re-layouts  5 us (6%)
    pallas_call x1, Pallas kernels, per_device(): pl.pallas_call(functools.partial(exchange, n), out_shape=pltpu.VMEM((n, 2...  80.3 us
    unnamed x12, local copies, waits for them, and re-layouts  5 us
    pallas_call x1, Pallas kernels, per_device(): pl.pallas_call(functools.partial(place, n), out_shape=jax.ShapeDtypeStruc...  4.29 us

profile of v2, /device:TPU:1, one launch (start us, length us, event | category | flops | bytes accessed | tf_op | source)
XLA Modules:
  0.0 89.6 jit_solution(4042076375429647201)
XLA Ops:
  0.0 0.0 copy-start
  0.0 1.3 %copy-done = bf16[96,3,2048]{2,0,1:T(8,128)(2,1)S(1)} copy-done((bf16[96,3,2048]{2,0,1:T(8,128)(2,1)S(1)}, bf16[96,3,2048]{2,0,1:T(8,128)(2,1)}, u32[]{:S(2)}) %copy-start) | copy-done | bytes 1179672
  1.3 0.0 copy-start.1
  1.3 1.0 %copy-done.1 = bf16[32,3,2048]{2,0,1:T(8,128)(2,1)S(1)} copy-done((bf16[32,3,2048]{2,0,1:T(8,128)(2,1)S(1)}, bf16[32,3,2048]{2,0,1:T(8,128)(2,1)}, u32[]{:S(2)}) %copy-start.1) | copy-done | bytes 393240
  2.3 0.0 copy-start.2
  2.3 0.7 copy-done.2
  3.0 0.0 copy-start.3
  3.0 0.7 copy-done.3
  3.7 0.0 copy-start.4
  3.7 0.7 copy-done.4
  4.4 0.0 copy-start.5
  4.4 0.7 copy-done.5
  5.0 80.3 %shard_map.64.products = bf16[16,2,3,96,512]{4,3,2,1,0:T(8,128)(2,1)S(1)} custom-call(bf16[3,96,2048]{2,1,0:T(8,128)(2,1)S(1)} %bitcast.2, bf16[3,32,2048]{2,1,0:T(8,128)(2,1)S(1)} %bitcast.3, s32[3,12,16]{2,1,0:T(8,128)S(1)} %copy-done.2, s32[3,4,16]{2,1,0:T(4,128)S(1)} %copy-done.3, s32[16]{0:T(128)S(1)} %copy-done.4, s32[16]{0:T(128)S(1)} %copy-done.5), custom_call_target="tpu_custom_call" | custom-call | tf_op jit(solution)/shard_map/pallas_call | solution.py:197
  85.3 4.3 %shard_map.65 = bf16[2,3,1536,512]{3,2,1,0:T(8,128)(2,1)} custom-call(s32[16]{0:T(128)S(1)} %copy-done.4, bf16[16,2,3,96,512]{4,3,2,1,0:T(8,128)(2,1)S(1)} %shard_map.64.products), custom_call_target="tpu_custom_call" | custom-call | tf_op jit(solution)/shard_map/pallas_call | solution.py:228
Async XLA Ops:
  0.0 1.3 %copy-start = (bf16[96,3,2048]{2,0,1:T(8,128)(2,1)S(1)}, bf16[96,3,2048]{2,0,1:T(8,128)(2,1)}, u32[]{:S(2)}) copy-start(bf16[96,3,2048]{2,0,1:T(8,128)(2,1)} %param.6) | copy-start | bytes 3538948
  1.3 1.0 %copy-start.1 = (bf16[32,3,2048]{2,0,1:T(8,128)(2,1)S(1)}, bf16[32,3,2048]{2,0,1:T(8,128)(2,1)}, u32[]{:S(2)}) copy-start(bf16[32,3,2048]{2,0,1:T(8,128)(2,1)} %param.7) | copy-start | bytes 1179652
  2.3 0.7 copy-start.2
  3.0 0.7 copy-start.3
  3.7 0.7 copy-start.4
  4.4 0.7 copy-start.5

commit v3 on v2

--- a/solution.py
+++ b/solution.py
@@ -10,7 +10,8 @@
 
 BLK = 128
 LANES = 128
-ORDER = 1
+STRIDE = 2
+SPARE = 2**19
 MESH = pl.DeviceIdType.MESH
 VMEM = pl.BlockSpec(memory_space=pltpu.VMEM)
 SMEM = pl.BlockSpec(memory_space=pltpu.SMEM)
@@ -25,8 +26,8 @@
 
 
 def exchange(
-    n, q_hbm, k_hbm, qe_ref, ke_ref, shard_ref, owner_ref, out_ref,
-    q_in, k_in, q_scaled, k_scaled, q_send, k_send, q_recv, k_recv, k_file,
+    n, q_hbm, k_hbm, qe_hbm, ke_hbm, shard_hbm, owner_hbm, out_ref,
+    qe_ref, ke_ref, shard_ref, owner_ref, q_in, k_in, q_scaled, k_scaled, q_send, k_send, q_recv, k_recv, k_file,
     in_sem, q_send_sem, k_send_sem, q_recv_sem, k_recv_sem,
 ):
     half = n // 2
@@ -37,10 +38,6 @@
     mine = me - lower
     other = half - mine
 
-    loads = [pltpu.make_async_copy(k_hbm, k_in, in_sem.at[0]), pltpu.make_async_copy(q_hbm, q_in, in_sem.at[1])]
-    for load in loads:
-        load.start()
-
     barrier = pltpu.get_barrier_semaphore()
 
     def greet(i, carry):
@@ -49,6 +46,18 @@
 
     lax.fori_loop(1, n, greet, 0)
 
+    def load(at, source, target):
+        copy = pltpu.make_async_copy(source, target, in_sem.at[at])
+        copy.start()
+        return copy
+
+    k_load = load(0, k_hbm, k_in)
+    shard_load = load(1, shard_hbm, shard_ref)
+    ke_load = load(2, ke_hbm, ke_ref)
+    owner_load = load(3, owner_hbm, owner_ref)
+    qe_load = load(4, qe_hbm, qe_ref)
+    q_load = load(5, q_hbm, q_in)
+    shard_load.wait()
     shard = shard_ref[me]
 
     def weigh(source, exps_ref, target, rows, head):
@@ -71,16 +80,9 @@
         weigh(q_in, qe_ref, q_scaled, q_rows, head)
         return carry
 
-    loads[0].wait()
-    lax.fori_loop(0, n, weigh_k, 0)
-    loads[1].wait()
-    lax.fori_loop(0, n, weigh_q, 0)
-
-    def prepare(t):
+    def prepare(scaled, send, t):
         for slot in range(2):
-            head = position(owner_ref, n, t + slot * half)
-            k_send[t, slot] = k_scaled[head]
-            q_send[t, slot] = q_scaled[head]
+            send[t, slot] = scaled[position(owner_ref, n, t + slot * half)]
 
     def copy(send, recv, send_sem, recv_sem, to, slot):
         return pltpu.make_async_remote_copy(
@@ -95,40 +97,42 @@
     q_copy = functools.partial(copy, q_send, q_recv, q_send_sem, q_recv_sem)
     k_copy = functools.partial(copy, k_send, k_recv, k_send_sem, k_recv_sem)
 
-    prepare(lower)
+    ke_load.wait()
+    k_load.wait()
+    lax.fori_loop(0, n, weigh_k, 0)
+    owner_load.wait()
+    prepare(k_scaled, k_send, lower)
     pl.semaphore_wait(barrier, n - 1)
     k_copy(lower + other, me).start()
+    k_recv[me] = k_send[lower]
+
+    def apart(i):
+        return lax.rem(i * STRIDE, half) + i * STRIDE // half
+
+    def k_step(i, carry):
+        t = lax.rem(lower + apart(i), half)
+        prepare(k_scaled, k_send, t)
+        k_copy(t + other, me).start()
+        k_copy(t + mine, me).start()
+        return carry
+
+    lax.fori_loop(1, half, k_step, 0)
+
+    qe_load.wait()
+    q_load.wait()
+    lax.fori_loop(0, n, weigh_q, 0)
+    prepare(q_scaled, q_send, lower)
     q_copy(lower + other, me).start()
-    k_recv[me] = k_send[lower]
     q_recv[me] = q_send[lower]
 
-    def far(i, carry):
-        t = lax.rem(lower + i, half)
-        prepare(t)
-        k_copy(t + other, me).start()
-        if ORDER == 0:
-            q_copy(t + other, me).start()
-        if ORDER == 1:
-            k_copy(t + mine, me).start()
-            q_copy(t + other, me).start()
-            q_copy(t + mine, me).start()
-        if ORDER == 2:
-            k_copy(t + mine, me).start()
-        return carry
-
-    lax.fori_loop(1, half, far, 0)
-
-    def near(i, carry):
-        t = lax.rem(lower + i, half)
-        if ORDER == 2:
-            q_copy(t + other, me).start()
-        if ORDER == 0:
-            k_copy(t + mine, me).start()
+    def q_step(i, carry):
+        t = lax.rem(lower + apart(i), half)
+        prepare(q_scaled, q_send, t)
+        q_copy(t + other, me).start()
         q_copy(t + mine, me).start()
         return carry
 
-    if ORDER != 1:
-        lax.fori_loop(1, half, near, 0)
+    lax.fori_loop(1, half, q_step, 0)
 
     def k_arrival(i, carry):
         k_copy(0, lax.rem(me + i, n)).wait_recv()
@@ -152,8 +156,8 @@
                 ).astype(jnp.bfloat16)
 
     def arrival(i, carry):
-        here = mine + lax.rem(lower + half - i, half)
-        there = other + lax.rem(lower + half - i, half)
+        here = mine + lax.rem(lower + half - apart(i), half)
+        there = other + lax.rem(lower + half - apart(i), half)
 
         @pl.when(i > 0)
         def _():
@@ -177,15 +181,12 @@
 
 def place(n, shard_ref, products, out_ref, sem):
     rows = products.shape[3]
-
-    def row_copy(host):
+    for host in range(n):
         at = pl.ds(pl.multiple_of(shard_ref[host] * rows, rows), rows)
-        return pltpu.make_async_copy(products.at[host], out_ref.at[:, :, at, :], sem.at[host])
-
-    for host in range(n):
-        row_copy(host).start()
-    for host in range(n):
-        row_copy(host).wait()
+        for slot in range(2):
+            for layer in range(products.shape[2]):
+                pltpu.make_async_copy(products.at[host, slot, layer], out_ref.at[slot, layer, at], sem).start()
+    pltpu.make_async_copy(out_ref, out_ref, sem).wait()
 
 
 def per_device(n, q_codes, k_codes, q_exps, k_exps, shard_of_host, head_owner):
@@ -194,12 +195,17 @@
     half = n // 2
     q_all, k_all = n * q_rows, n * k_rows
     sent = jnp.bfloat16
+    held = n * 2 * layers * -(-q_rows // 16) * 16 * k_all * 2
     products = pl.pallas_call(
         functools.partial(exchange, n),
         out_shape=pltpu.VMEM((n, 2, layers, q_rows, k_all), jnp.bfloat16),
-        in_specs=[HBM, HBM, SMEM, SMEM, SMEM, SMEM],
+        in_specs=[HBM] * 6,
         out_specs=VMEM,
         scratch_shapes=[
+            pltpu.SMEM(q_exps.shape, jnp.int32),
+            pltpu.SMEM(k_exps.shape, jnp.int32),
+            pltpu.SMEM((n,), jnp.int32),
+            pltpu.SMEM((n,), jnp.int32),
             pltpu.VMEM((layers, q_rows, width), sent),
             pltpu.VMEM((layers, k_rows, width), sent),
             pltpu.VMEM((n, layers, q_rows, LANES), sent),
@@ -209,14 +215,14 @@
             pltpu.VMEM((n, 2, layers, q_rows, LANES), sent),
             pltpu.VMEM((n, 2, layers, k_rows, LANES), sent),
             pltpu.VMEM((2, layers, k_all, LANES), sent),
-            pltpu.SemaphoreType.DMA((2,)),
+            pltpu.SemaphoreType.DMA((6,)),
             pltpu.SemaphoreType.DMA((n,)),
             pltpu.SemaphoreType.DMA((n,)),
             pltpu.SemaphoreType.DMA((n,)),
             pltpu.SemaphoreType.DMA((n,)),
         ],
         compiler_params=pltpu.CompilerParams(
-            collective_id=0, has_side_effects=True, vmem_limit_bytes=40 * 2**20
+            collective_id=0, has_side_effects=True, vmem_limit_bytes=64 * 2**20 - held - SPARE
         ),
     )(q_codes.transpose(1, 0, 2), k_codes.transpose(1, 0, 2), q_exps, k_exps, shard_of_host, head_owner)
 
@@ -230,7 +236,7 @@
         out_shape=jax.ShapeDtypeStruct((2, layers, q_all, k_all), jnp.bfloat16),
         in_specs=[SMEM, VMEM],
         out_specs=HBM,
-        scratch_shapes=[pltpu.SemaphoreType.DMA((n,))],
+        scratch_shapes=[pltpu.SemaphoreType.DMA],
         compiler_params=pltpu.CompilerParams(vmem_limit_bytes=40 * 2**20),
     )(shard_of_host, products)
 

time: 90.2 us -> 80.4 us (0.89)
  local copies, waits for them, and re-layouts: 5 us -> 0.01 us
  Pallas kernels: 84.6 us -> 79.8 us
    unnamed x12 -> x2, local copies, waits for them, and re-layouts: 5 us -> 0.01 us
    pallas_call x1, Pallas kernels: 80.3 us -> 75.7 us  [per_device(): pl.pallas_call(functools.partial(exchange, n), out_shape=pltpu.VMEM((n, 2...]
where the time goes in v3:
time: 80.4 us; the launch traced here: 79.8 us
  Pallas kernels  79.8 us (99%)
    pallas_call x1, Pallas kernels, per_device(): pl.pallas_call(functools.partial(exchange, n), out_shape=pltpu.VMEM((n, 2...  75.7 us
    pallas_call x1, Pallas kernels, per_device(): pl.pallas_call(functools.partial(place, n), out_shape=jax.ShapeDtypeStruc...  4.11 us

profile of v3, /device:TPU:1, one launch (start us, length us, event | category | flops | bytes accessed | tf_op | source)
XLA Modules:
  0.0 79.8 jit_solution(13417309714829706405)
XLA Ops:
  0.0 0.0 copy-start
  0.0 75.7 %shard_map.64.products = bf16[16,2,3,96,512]{4,3,2,1,0:T(8,128)(2,1)S(1)} custom-call(bf16[3,96,2048]{2,1,0:T(8,128)(2,1)} %bitcast.2, bf16[3,32,2048]{2,1,0:T(8,128)(2,1)} %bitcast.3, s32[3,12,16]{2,1,0:T(8,128)} %qe_hbm.1, s32[3,4,16]{2,1,0:T(4,128)} %ke_hbm.1, s32[16]{0:T(128)} %shard_ref.1, s32[16]{0:T(128)} %owner_hbm.1), custom_call_target="tpu_custom_call" | custom-call | tf_op jit(solution)/shard_map/pallas_call | solution.py:199
  75.7 0.0 copy-done
  75.7 4.1 %shard_map.65 = bf16[2,3,1536,512]{3,2,1,0:T(8,128)(2,1)} custom-call(s32[16]{0:T(128)S(1)} %copy-done, bf16[16,2,3,96,512]{4,3,2,1,0:T(8,128)(2,1)S(1)} %shard_map.64.products), custom_call_target="tpu_custom_call" | custom-call | tf_op jit(solution)/shard_map/pallas_call | solution.py:234
Async XLA Ops:
  0.0 75.7 %copy-start = (s32[16]{0:T(128)S(1)}, s32[16]{0:T(128)}, u32[]{:S(2)}) copy-start(s32[16]{0:T(128)} %shard_ref.1) | copy-start | bytes 196

commit v4 on v3

--- a/solution.py
+++ b/solution.py
@@ -136,6 +136,7 @@
 
     def k_arrival(i, carry):
         k_copy(0, lax.rem(me + i, n)).wait_recv()
+        k_copy(lax.rem(me + i, n), 0).wait_send()
         return carry
 
     lax.fori_loop(1, n, k_arrival, 0)
@@ -172,7 +173,6 @@
 
     def finish(i, carry):
         peer = lax.rem(me + i, n)
-        k_copy(peer, 0).wait_send()
         q_copy(peer, 0).wait_send()
         return carry
 

time: 80.4 us -> 80.4 us (level)
  no operation moved by 1% of the time
where the time goes in v4:
time: 80.4 us; the launch traced here: 79.8 us
  Pallas kernels  79.7 us (99%)
    pallas_call x1, Pallas kernels, per_device(): pl.pallas_call(functools.partial(exchange, n), out_shape=pltpu.VMEM((n, 2...  75.6 us
    pallas_call x1, Pallas kernels, per_device(): pl.pallas_call(functools.partial(place, n), out_shape=jax.ShapeDtypeStruc...  4.11 us

profile of v4, /device:TPU:1, one launch (start us, length us, event | category | flops | bytes accessed | tf_op | source)
XLA Modules:
  0.0 79.8 jit_solution(1609951962259961556)
XLA Ops:
  0.0 0.0 copy-start
  0.0 75.6 %shard_map.64.products = bf16[16,2,3,96,512]{4,3,2,1,0:T(8,128)(2,1)S(1)} custom-call(bf16[3,96,2048]{2,1,0:T(8,128)(2,1)} %bitcast.2, bf16[3,32,2048]{2,1,0:T(8,128)(2,1)} %bitcast.3, s32[3,12,16]{2,1,0:T(8,128)} %qe_hbm.1, s32[3,4,16]{2,1,0:T(4,128)} %ke_hbm.1, s32[16]{0:T(128)} %shard_ref.1, s32[16]{0:T(128)} %owner_hbm.1), custom_call_target="tpu_custom_call" | custom-call | tf_op jit(solution)/shard_map/pallas_call | solution.py:199
  75.6 0.0 copy-done
  75.7 4.1 %shard_map.65 = bf16[2,3,1536,512]{3,2,1,0:T(8,128)(2,1)} custom-call(s32[16]{0:T(128)S(1)} %copy-done, bf16[16,2,3,96,512]{4,3,2,1,0:T(8,128)(2,1)S(1)} %shard_map.64.products), custom_call_target="tpu_custom_call" | custom-call | tf_op jit(solution)/shard_map/pallas_call | solution.py:234
Async XLA Ops:
  0.0 75.7 %copy-start = (s32[16]{0:T(128)S(1)}, s32[16]{0:T(128)}, u32[]{:S(2)}) copy-start(s32[16]{0:T(128)} %shard_ref.1) | copy-start | bytes 196
